TPU v7x, 32 devices: a whole 2x2x4 slice. The times are simulated.
32 devices in a mesh: row: 8 (over y, x, core), col: 4 (over z).
Axes of the slice: x: 2, y: 2, z: 4, core: 2. Of those that a mesh axis runs over, the one named last changes fastest.
Arguments:
- eigvecs: float32 [38400, 2560], P('row', 'col'), may hold values from -6 to 6
- panels: float32 [2, 38400, 128], P(None, 'row', 'col'), may hold values from -0.125 to 0.125
- factors: float32 [2, 128, 128], replicated, may hold values from -1 to 1, as said below
Outputs:
- rotated: float32 [38400, 2560], P('row', 'col')
Inputs may be any that keep to these rules, and one draw needn't show every extreme that they name: `factors`: each factor is upper triangular with a positive diagonal.
All inputs are finite; a program needn't handle non-finite values.
Results may differ from a plain program's by a relative error of at most 0.0001.
Values sent between devices are 32-bit elements; how exact they have to be, the bound alone decides.
A program may use at most 64 MiB of HBM per device.

v0:
```python
import jax
import jax.numpy as jnp
from jax import lax
from jax.sharding import PartitionSpec as P


def inner(left, right):
    return lax.dot_general(
        left,
        right,
        (((0,), (0,)), ((), ())),
        precision=lax.Precision.HIGHEST,
        preferred_element_type=jnp.float32,
    )


def times(left, right):
    return jnp.dot(left, right, precision=lax.Precision.HIGHEST, preferred_element_type=jnp.float32)


def per_device(eigvecs, panels, factors):
    rotated = eigvecs
    for index in range(panels.shape[0]):
        vectors = lax.all_gather(panels[index], "col", axis=1, tiled=True)
        projection = lax.psum(inner(vectors, rotated), "row")
        scaled = times(factors[index], projection)
        rotated = rotated - times(vectors, scaled)
    return rotated


def solution(mesh):
    return jax.shard_map(
        per_device,
        mesh=mesh,
        in_specs=(P("row", "col"), P(None, "row", "col"), P()),
        out_specs=P("row", "col"),
        check_vma=False,
    )
```

profile of v0, /device:TPU:0, one launch (start us, length us, event | category | flops | bytes accessed | tf_op | source)
XLA Modules:
  0.0 284.0 jit_solution(684351851440689307)
XLA Ops:
  6.5 0.0 all-gather.5.cloned.1.call-start
  6.5 2.4 fusion.15
  8.9 0.0 all-gather.5.cloned.1.call-update
  8.9 0.0 copy-start.2
  8.9 0.0 all-reduce.3.cloned.1.call-start
  9.0 55.4 %all-gather.5.cloned.1.call-done = f32[1,4800,128]{1,2,0:T(8,128)} async-done(((f32[1,4800,32]{1,2,0:T(8,128)}), f32[1,4800,128]{1,2,0:T(8,128)}) %all-gather.5.cloned.1.call-update) | async-done | bytes 2457616 | tf_op jit(solution)/shard_map/all_gather | solution.py:24
  64.4 0.0 copy-start
  64.4 12.1 %fusion.4 = f32[128,640]{1,0:T(8,128)} fusion(f32[4800,640]{1,0:T(8,128)} %param.3, f32[1,4800,128]{1,2,0:T(8,128)} %all-gather.5.cloned.1.call-done), kind=kOutput, calls=%fused_computation.6 | convolution fusion | flops 4718592000 | bytes 15073280 | tf_op jit(solution)/shard_map/dot_general | solution.py:8
  76.6 0.0 all-reduce.3.cloned.1.call-update
  76.6 0.0 all-gather.7.cloned.1.call-start
  76.6 0.7 all-gather.7.cloned.1.call-update
  77.3 0.0 all-reduce.5.cloned.1.call-start
  77.4 52.1 %all-reduce.3.cloned.1.call-done = f32[128,640]{1,0:T(8,128)} async-done(((f32[128,640]{1,0:T(8,128)}), f32[128,640]{1,0:T(8,128)}) %all-reduce.3.cloned.1.call-update) | async-done | bytes 327696 | tf_op jit(solution)/shard_map/psum | solution.py:25
  129.4 0.0 copy-done.2
  129.4 1.7 fusion.11
  131.1 0.0 copy-done
  131.1 16.2 %bitcast_subtract_fusion.1 = f32[4800,640]{1,0:T(8,128)} fusion(f32[4800,640]{1,0:T(8,128)} %param.3, f32[640,128]{1,0:T(8,128)S(1)} %fusion.11, f32[1,4800,128]{1,2,0:T(8,128)S(1)} %copy-done), kind=kOutput, calls=%fused_computation.1 | convolution fusion | flops 4721664000 | bytes 27361280 | tf_op jit(solution)/shard_map/dot_general | solution.py:18
  147.3 35.8 %all-gather.7.cloned.1.call-done = f32[1,4800,128]{1,2,0:T(8,128)} async-done(((f32[1,4800,32]{1,2,0:T(8,128)}), f32[1,4800,128]{1,2,0:T(8,128)}) %all-gather.7.cloned.1.call-update) | async-done | bytes 2457616 | tf_op jit(solution)/shard_map/all_gather | solution.py:24
  183.1 23.7 %fusion.6 = f32[128,640]{0,1:T(8,128)} fusion(f32[4800,640]{1,0:T(8,128)} %bitcast_subtract_fusion.1, f32[1,4800,128]{1,2,0:T(8,128)} %all-gather.7.cloned.1.call-done), kind=kOutput, calls=%fused_computation.8 | convolution fusion | flops 4718592000 | bytes 15073280 | tf_op jit(solution)/shard_map/dot_general | solution.py:8
  206.8 0.0 all-reduce.5.cloned.1.call-update
  206.8 52.8 %all-reduce.5.cloned.1.call-done = f32[128,640]{0,1:T(8,128)} async-done(((f32[128,640]{0,1:T(8,128)}), f32[128,640]{0,1:T(8,128)}) %all-reduce.5.cloned.1.call-update) | async-done | bytes 327696 | tf_op jit(solution)/shard_map/psum | solution.py:25
  259.6 1.4 fusion.9
  261.1 0.0 copy-done.1
  261.1 16.4 %bitcast_subtract_fusion = f32[4800,640]{1,0:T(8,128)} fusion(f32[4800,640]{1,0:T(8,128)} %bitcast_subtract_fusion.1, f32[640,128]{1,0:T(8,128)S(1)} %fusion.9, f32[1,4800,128]{1,2,0:T(8,128)S(1)} %copy-done.1), kind=kOutput, calls=%fused_computation | convolution fusion | flops 4721664000 | bytes 27361280 | tf_op jit(solution)/shard_map/dot_general | solution.py:18
  (1 shorter events, 0.0 us)
Async XLA Ops:
  6.5 57.9 %all-gather.5.cloned.1.call-start = ((), (), s32[]{:S(2)}) async-start(), calls=%async_computation.2 | async-start | bytes 3112960 | tf_op jit(solution)/shard_map/all_gather | solution.py:24
  8.9 120.5 %copy-start.2 = (f32[2,128,128]{2,1,0:T(8,128)S(1)}, f32[2,128,128]{2,1,0:T(8,128)}, u32[]{:S(2)}) copy-start(f32[2,128,128]{2,1,0:T(8,128)} %param.5) | copy-start | bytes 393220
  8.9 120.5 %all-reduce.3.cloned.1.call-start = ((), (), s32[]{:S(2)}) async-start(), calls=%async_computation | async-start | bytes 655360 | tf_op jit(solution)/shard_map/psum | solution.py:25
  64.4 66.7 %copy-start = (f32[1,4800,128]{1,2,0:T(8,128)S(1)}, f32[1,4800,128]{1,2,0:T(8,128)}, u32[]{:S(2)}) copy-start(f32[1,4800,128]{1,2,0:T(8,128)} %all-gather.5.cloned.1.call-done) | copy-start | bytes 7372804
  76.6 106.5 %all-gather.7.cloned.1.call-start = ((), (), s32[]{:S(2)}) async-start(), calls=%async_computation.3 | async-start | bytes 3112960 | tf_op jit(solution)/shard_map/all_gather | solution.py:24
  77.3 182.3 %all-reduce.5.cloned.1.call-start = ((), (), s32[]{:S(2)}) async-start(), calls=%async_computation.1 | async-start | bytes 655360 | tf_op jit(solution)/shard_map/psum | solution.py:25
  183.1 78.0 %copy-start.1 = (f32[1,4800,128]{1,2,0:T(8,128)S(1)}, f32[1,4800,128]{1,2,0:T(8,128)}, u32[]{:S(2)}) copy-start(f32[1,4800,128]{1,2,0:T(8,128)} %all-gather.7.cloned.1.call-done) | copy-start | bytes 7372804
Sparse Core Ops, SparseCore 0:
  9.1 55.3 all-gather.4
  76.7 52.6 all-reduce.2
  131.0 52.0 all-gather.6
  206.9 52.6 all-reduce.4
where the time goes:
time: 284 us
  waiting for transfers between devices  197 us (69%)
  matrix products  71.4 us (25%)
  between operations  13.2 us (5%)
    psum x2, waiting for transfers between devices, per_device(): projection = lax.psum(inner(vectors, rotated), 'row')  105 us
    all_gather x2, waiting for transfers between devices, per_device(): vectors = lax.all_gather(panels[index], 'col', axis=1, tiled=True)  91.3 us
    dot_general x2, matrix products, inner(): lax.dot_general(left, right, (((0,), (0,)), ((), ())), precision=lax.Prec...  35.8 us
    dot_general x4, matrix products, times(): jnp.dot(left, right, precision=lax.Precision.HIGHEST, preferred_element_t...  35.6 us
  transfers between devices with their start and end apart: 4, of which 4 were waited for; matrix products, arithmetic and copies ran while one was open for 6% of the time, Pallas kernels for 0%

commit v1 on v0

v1 whole, which is shorter than its diff:
```python
import functools

import jax
import jax.numpy as jnp
from jax import lax
from jax.experimental import pallas as pl
from jax.experimental.pallas import tpu as pltpu
from jax.sharding import PartitionSpec as P

MESH = pl.DeviceIdType.MESH
PIECE = 16
DEPTH = 768
F32 = jnp.float32
BF16 = jnp.bfloat16


def halves(value):
    high = value.astype(BF16)
    return high, (value - high.astype(F32)).astype(BF16)


def rows_by(left, right):
    return lax.dot_general(left, right, (((1,), (1,)), ((), ())), preferred_element_type=F32)


def plain(left, right):
    return lax.dot_general(left, right, (((1,), (0,)), ((), ())), preferred_element_type=F32)


def exact(left, right):
    return jnp.dot(left, right, precision=lax.Precision.HIGHEST, preferred_element_type=F32)


def gather_kernel(
    peers, line, step, own_ref, x_ref, factors_ref, vh_out, vl_out, sh_ref, sl_ref,
    vt, vh, vl, xh, xl, stage, part0, part1, got0, got1, small, final,
    own_sem, x_sem, out_sem, left_sem, right_sem, recv_sem, put_sem, got_sem,
):
    row, col = lax.axis_index("row"), lax.axis_index("col")
    columns, count = own_ref.shape[1:]
    per = columns // PIECE
    width = x_ref.shape[1]
    panel_columns = vh.shape[1]
    full = count // DEPTH
    parts, gots = (part0, part1), (got0, got1)

    own_copy = pltpu.make_async_copy(own_ref, vt.at[col], own_sem)
    own_copy.start()

    def fetch(block):
        slot = lax.rem(block, 2)
        return pltpu.make_async_copy(x_ref.at[pl.ds(pl.multiple_of(block * step, step), step)], stage.at[slot], x_sem.at[slot])

    fetch(0).start()

    barrier = pltpu.get_barrier_semaphore()
    for offset in range(1, peers):
        pl.semaphore_signal(barrier, inc=1, device_id=(lax.rem(row + offset, peers), col), device_id_type=MESH)

    @pl.when(col > 0)
    def _():
        pl.semaphore_signal(barrier, inc=1, device_id=(row, col - 1), device_id_type=MESH)

    @pl.when(col < line - 1)
    def _():
        pl.semaphore_signal(barrier, inc=1, device_id=(row, col + 1), device_id_type=MESH)

    pl.semaphore_wait(barrier, peers - 1 + jnp.where(col > 0, 1, 0) + jnp.where(col < line - 1, 1, 0))

    def move(source, origin, panel, half, sems, away, target):
        place = pl.ds(pl.multiple_of(half * PIECE, PIECE), PIECE)
        return pltpu.make_async_remote_copy(
            src_ref=source.at[panel, place],
            dst_ref=vt.at[origin, panel, place],
            send_sem=sems.at[away, panel, half],
            recv_sem=recv_sem.at[origin, panel, half],
            device_id=(row, target),
            device_id_type=MESH,
        )

    def own_sends(act):
        for panel in range(2):
            for half in range(per):
                @pl.when(col > 0)
                def _():
                    act(move(own_ref, col, panel, half, left_sem, 0, col - 1))

                @pl.when(col < line - 1)
                def _():
                    act(move(own_ref, col, panel, half, right_sem, 0, col + 1))

    own_sends(lambda copy: copy.start())

    blocks = count // step

    @pl.loop(0, blocks)
    def _(block):
        @pl.when(block + 1 < blocks)
        def _():
            fetch(block + 1).start()

        fetch(block).wait()
        place = pl.ds(pl.multiple_of(block * step, step), step)
        high, low = halves(stage[lax.rem(block, 2)])
        xh[place] = high
        xl[place] = low

    own_copy.wait()

    def process(origin, panel, half):
        index = origin * per + half
        place = pl.ds(pl.multiple_of(index * PIECE, PIECE), PIECE)
        part = parts[panel]
        vt_place = pl.ds(pl.multiple_of(half * PIECE, PIECE), PIECE)
        part[index] = jnp.zeros(part.shape[1:], F32)

        def block(lanes, rows):
            high, low = halves(vt[origin, panel, vt_place, lanes])
            vh[panel, place, lanes] = high
            vl[panel, place, lanes] = low
            both = jnp.concatenate([high, low], axis=0)
            first = plain(both, xh[rows])
            second = plain(high, xl[rows])
            part[index, :, :width] += first[:PIECE] + first[PIECE:] + second
            if panel == 1:
                third = rows_by(both, vh[0, :, lanes])
                fourth = rows_by(high, vl[0, :, lanes])
                part[index, :, width:] += third[:PIECE] + third[PIECE:] + fourth

        @pl.loop(0, full)
        def _(number):
            place = pl.ds(pl.multiple_of(number * DEPTH, DEPTH), DEPTH)
            block(place, place)

        if count % DEPTH:
            rest = pl.ds(full * DEPTH, count - full * DEPTH)
            block(rest, rest)

        @pl.loop(1, peers)
        def _(offset):
            pltpu.make_async_remote_copy(
                src_ref=part.at[index],
                dst_ref=gots[panel].at[index, offset - 1],
                send_sem=put_sem.at[panel, index],
                recv_sem=got_sem.at[panel, index],
                device_id=(lax.rem(row + offset, peers), col),
                device_id_type=MESH,
            ).start()

    def arrivals(panel):
        @pl.loop(1, line)
        def _(away):
            right, left = col + away, col - away

            @pl.loop(0, per)
            def _(half):
                @pl.when(right < line)
                def _():
                    move(own_ref, right, panel, half, left_sem, away, col).wait_recv()

                    @pl.when(col > 0)
                    def _():
                        move(vt.at[right], right, panel, half, left_sem, away, col - 1).start()

                @pl.when(left >= 0)
                def _():
                    move(own_ref, left, panel, half, right_sem, away, col).wait_recv()

                    @pl.when(col < line - 1)
                    def _():
                        move(vt.at[left], left, panel, half, right_sem, away, col + 1).start()

                @pl.when(right < line)
                def _():
                    process(right, panel, half)

                @pl.when(left >= 0)
                def _():
                    process(left, panel, half)

    def own_pieces(panel):
        @pl.loop(0, per)
        def _(half):
            process(col, panel, half)

    def save(panel):
        return (
            pltpu.make_async_copy(vh.at[panel], vh_out.at[panel], out_sem.at[panel, 0]),
            pltpu.make_async_copy(vl.at[panel], vl_out.at[panel], out_sem.at[panel, 1]),
        )

    def collect(panel, keep):
        part, got = parts[panel], gots[panel]

        @pl.loop(0, line * per)
        def _(index):
            pltpu.make_async_copy(got.at[index], got.at[index], got_sem.at[panel, index]).wait()
            total = part[index]
            for offset in range(peers - 1):
                total = total + got[index, offset]
            keep[pl.ds(pl.multiple_of(index * PIECE, PIECE), PIECE)] = total

    def emit(panel, scaled):
        high, low = halves(scaled)
        sh_ref[panel] = high
        sl_ref[panel] = low

    own_pieces(0)
    arrivals(0)
    for copy in save(0):
        copy.start()
    own_pieces(1)
    collect(0, small)
    scaled = exact(factors_ref[0], small[...])
    emit(0, scaled)
    small[...] = scaled
    arrivals(1)
    for copy in save(1):
        copy.start()

    collect(1, final)
    projection = final[:, :width] - exact(final[:, width:], small[...])
    emit(1, exact(factors_ref[1], projection))

    own_sends(lambda copy: copy.wait_send())
    for panel in range(2):
        @pl.loop(1, line)
        def _(away):
            @pl.loop(0, per)
            def _(half):
                @pl.when(jnp.logical_and(col + away < line, col > 0))
                def _():
                    move(own_ref, col + away, panel, half, left_sem, away, col - 1).wait_send()

                @pl.when(jnp.logical_and(col - away >= 0, col < line - 1))
                def _():
                    move(own_ref, col - away, panel, half, right_sem, away, col + 1).wait_send()

        @pl.loop(0, line * per)
        def _(index):
            got = gots[panel]
            pltpu.make_async_copy(got.at[index], got.at[index], put_sem.at[panel, index]).wait()

        for copy in save(panel):
            copy.wait()


def update_kernel(x_ref, vh_ref, vl_ref, sh_ref, sl_ref, out_ref):
    def product(left, right):
        return lax.dot_general(left, right, (((0,), (0,)), ((), ())), preferred_element_type=F32)

    high = vh_ref[...]
    out_ref[...] = x_ref[...] - (
        product(high, sh_ref[...]) + product(vl_ref[...], sh_ref[...]) + product(high, sl_ref[...])
    )


def per_device(peers, line, eigvecs, panels, factors):
    count, width = eigvecs.shape
    columns = panels.shape[2]
    total = columns * line
    per = columns // PIECE
    step = 480 if count % 480 == 0 else PIECE
    own = jnp.swapaxes(panels, 1, 2)
    anywhere = pl.BlockSpec(memory_space=pl.ANY)
    inside = pl.BlockSpec(memory_space=pltpu.VMEM)
    pieces = line * per
    wide = width + total
    vh, vl, sh, sl = pl.pallas_call(
        functools.partial(gather_kernel, peers, line, step),
        out_shape=(
            jax.ShapeDtypeStruct((2, total, count), BF16),
            jax.ShapeDtypeStruct((2, total, count), BF16),
            jax.ShapeDtypeStruct((2, total, width), BF16),
            jax.ShapeDtypeStruct((2, total, width), BF16),
        ),
        in_specs=[anywhere, anywhere, inside],
        out_specs=(anywhere, anywhere, inside, inside),
        scratch_shapes=[
            pltpu.VMEM((line, 2, columns, count), F32),
            pltpu.VMEM((2, total, count), BF16),
            pltpu.VMEM((2, total, count), BF16),
            pltpu.VMEM((count, width), BF16),
            pltpu.VMEM((count, width), BF16),
            pltpu.VMEM((2, step, width), F32),
            pltpu.VMEM((pieces, PIECE, width), F32),
            pltpu.VMEM((pieces, PIECE, wide), F32),
            pltpu.VMEM((pieces, peers - 1, PIECE, width), F32),
            pltpu.VMEM((pieces, peers - 1, PIECE, wide), F32),
            pltpu.VMEM((total, width), F32),
            pltpu.VMEM((total, wide), F32),
            pltpu.SemaphoreType.DMA,
            pltpu.SemaphoreType.DMA((2,)),
            pltpu.SemaphoreType.DMA((2, 2)),
            pltpu.SemaphoreType.DMA((line, 2, per)),
            pltpu.SemaphoreType.DMA((line, 2, per)),
            pltpu.SemaphoreType.DMA((line, 2, per)),
            pltpu.SemaphoreType.DMA((2, pieces)),
            pltpu.SemaphoreType.DMA((2, pieces)),
        ],
        compiler_params=pltpu.CompilerParams(
            collective_id=0, has_side_effects=True, vmem_limit_bytes=44 * 1024 * 1024
        ),
        name="gather_project",
    )(own, eigvecs, factors)
    vh, vl, sh, sl = (array.reshape(2 * total, array.shape[2]) for array in (vh, vl, sh, sl))
    rows = min(640, count)
    tall = pl.BlockSpec((rows, width), lambda number: (number, 0))
    flat = pl.BlockSpec((2 * total, rows), lambda number: (0, number))
    fixed = pl.BlockSpec((2 * total, width), lambda number: (0, 0))
    return pl.pallas_call(
        update_kernel,
        out_shape=jax.ShapeDtypeStruct((count, width), F32),
        grid=(pl.cdiv(count, rows),),
        in_specs=[tall, flat, flat, fixed, fixed],
        out_specs=tall,
        compiler_params=pltpu.CompilerParams(vmem_limit_bytes=32 * 1024 * 1024),
        name="update",
    )(eigvecs, vh, vl, sh, sl)


def solution(mesh):
    return jax.shard_map(
        functools.partial(per_device, mesh.shape["row"], mesh.shape["col"]),
        mesh=mesh,
        in_specs=(P("row", "col"), P(None, "row", "col"), P()),
        out_specs=P("row", "col"),
        check_vma=False,
    )
```

time: 284 us -> 122 us (0.43)
  waiting for transfers between devices: 197 us -> 0 us
  Pallas kernels: 0 us -> 113 us
  matrix products: 71.4 us -> 0 us
  between operations: 13.2 us -> 0.02 us
  local copies, waits for them, and re-layouts: 2.39 us -> 8.51 us
    pallas_call x0 -> x2, Pallas kernels: none -> 113 us  [the longest x1 103 us: per_device(): pl.pallas_call(functools.partial(gather_kernel, peers, line, step), out_s...]
    psum x2 -> x0, waiting for transfers between devices: 105 us -> none  [per_device(): projection = lax.psum(inner(vectors, rotated), 'row')]
    all_gather x2 -> x0, waiting for transfers between devices: 91.3 us -> none  [per_device(): vectors = lax.all_gather(panels[index], 'col', axis=1, tiled=True)]
    dot_general x6 -> x0, matrix products: 71.4 us -> none  [the longest x2 35.8 us: inner(): lax.dot_general(left, right, (((0,), (0,)), ((), ())), precision=lax.Prec...]
    unnamed x6 -> x14, local copies, waits for them, and re-layouts: 0.01 us -> 8.51 us
  transfers between devices with their start and end apart: 4 -> 0, of which waited for: 4 -> 0; matrix products, arithmetic and copies ran while one was open for 6% -> 0% of each run, Pallas kernels for 0% -> 0%
where the time goes in v1:
time: 122 us; the launch traced here: 121 us
  Pallas kernels  113 us (93%)
  local copies, waits for them, and re-layouts  8.51 us (7%)
    pallas_call x1, Pallas kernels, per_device(): pl.pallas_call(functools.partial(gather_kernel, peers, line, step), out_s...  103 us
    pallas_call x1, Pallas kernels, per_device(): pl.pallas_call(update_kernel, out_shape=jax.ShapeDtypeStruct((count, widt...  9.87 us
    unnamed x14, local copies, waits for them, and re-layouts  8.51 us

profile of v1, /device:TPU:0, one launch (start us, length us, event | category | flops | bytes accessed | tf_op | source)
XLA Modules:
  0.0 121.3 jit_solution(3289900380834094337)
XLA Ops:
  0.0 0.0 copy-start.5
  0.0 1.3 %copy-done.5 = f32[2,4800,32]{1,2,0:T(8,128)S(1)} copy-done((f32[2,4800,32]{1,2,0:T(8,128)S(1)}, f32[2,4800,32]{1,2,0:T(8,128)}, u32[]{:S(2)}) %copy-start.5) | copy-done | bytes 1228824
  1.3 0.0 copy-start.6
  1.3 0.9 copy-done.6
  2.2 0.0 copy-start
  2.2 102.9 %gather_project.1 = (bf16[2,128,4800]{2,1,0:T(8,128)(2,1)S(1)}, bf16[2,128,4800]{2,1,0:T(8,128)(2,1)S(1)}, bf16[2,128,640]{2,1,0:T(8,128)(2,1)S(1)}, bf16[2,128,640]{2,1,0:T(8,128)(2,1)S(1)}) custom-call(f32[2,32,4800]{2,1,0:T(8,128)S(1)} %bitcast.7, f32[4800,640]{1,0:T(8,128)} %x_ref.3, f32[2,128,128]{2,1,0:T(8,128)S(1)} %copy-done.6), custom_call_target="tpu_custom_call" | custom-call | tf_op jit(solution)/shard_map/gather_project/pallas_call | solution.py:269
  105.1 0.0 copy-start.1
  105.1 1.4 %copy-done.1 = bf16[2,128,4800]{2,1,0:T(8,128)(2,1)} copy-done((bf16[2,128,4800]{2,1,0:T(8,128)(2,1)}, bf16[2,128,4800]{2,1,0:T(8,128)(2,1)S(1)}, u32[]{:S(2)}) %copy-start.1) | copy-done | bytes 2457624
  106.5 0.0 copy-start.3
  106.5 1.5 %copy-done.3 = bf16[2,128,4800]{2,1,0:T(8,128)(2,1)} copy-done((bf16[2,128,4800]{2,1,0:T(8,128)(2,1)}, bf16[2,128,4800]{2,1,0:T(8,128)(2,1)S(1)}, u32[]{:S(2)}) %copy-start.3) | copy-done | bytes 2457624
  108.0 0.0 copy-done
  108.0 0.0 copy-start.2
  108.0 1.7 %copy-done.2 = bf16[2,128,4800]{2,1,0:T(8,128)(2,1)S(1)} copy-done((bf16[2,128,4800]{2,1,0:T(8,128)(2,1)S(1)}, bf16[2,128,4800]{2,1,0:T(8,128)(2,1)}, u32[]{:S(2)}) %copy-start.2) | copy-done | bytes 2457624
  109.7 0.0 copy-start.4
  109.7 1.7 %copy-done.4 = bf16[2,128,4800]{2,1,0:T(8,128)(2,1)S(1)} copy-done((bf16[2,128,4800]{2,1,0:T(8,128)(2,1)S(1)}, bf16[2,128,4800]{2,1,0:T(8,128)(2,1)}, u32[]{:S(2)}) %copy-start.4) | copy-done | bytes 2457624
  111.4 9.9 %update.1 = f32[4800,640]{1,0:T(8,128)} custom-call(f32[4800,640]{1,0:T(8,128)S(1)} %copy-done, bf16[256,4800]{1,0:T(8,128)(2,1)S(1)} %bitcast.5, bf16[256,4800]{1,0:T(8,128)(2,1)S(1)} %bitcast.6, bf16[256,640]{1,0:T(8,128)(2,1)S(1)} %bitcast.8, bf16[256,640]{1,0:T(8,128)(2,1)S(1)} %bitcast.9), custom_call_target="tpu_custom_call" | custom-call | tf_op jit(solution)/shard_map/update/pallas_call | solution.py:311
Async XLA Ops:
  0.0 1.3 %copy-start.5 = (f32[2,4800,32]{1,2,0:T(8,128)S(1)}, f32[2,4800,32]{1,2,0:T(8,128)}, u32[]{:S(2)}) copy-start(f32[2,4800,32]{1,2,0:T(8,128)} %param.4) | copy-start | bytes 3686404
  1.3 0.9 copy-start.6
  2.2 105.8 %copy-start = (f32[4800,640]{1,0:T(8,128)S(1)}, f32[4800,640]{1,0:T(8,128)}, u32[]{:S(2)}) copy-start(f32[4800,640]{1,0:T(8,128)} %x_ref.3) | copy-start | bytes 36864004
  105.1 1.5 %copy-start.1 = (bf16[2,128,4800]{2,1,0:T(8,128)(2,1)}, bf16[2,128,4800]{2,1,0:T(8,128)(2,1)S(1)}, u32[]{:S(2)}) copy-start(bf16[2,128,4800]{2,1,0:T(8,128)(2,1)S(1)} %get-tuple-element.9) | copy-start | bytes 7372804
  106.5 1.5 %copy-start.3 = (bf16[2,128,4800]{2,1,0:T(8,128)(2,1)}, bf16[2,128,4800]{2,1,0:T(8,128)(2,1)S(1)}, u32[]{:S(2)}) copy-start(bf16[2,128,4800]{2,1,0:T(8,128)(2,1)S(1)} %get-tuple-element.10) | copy-start | bytes 7372804
  108.0 1.7 %copy-start.2 = (bf16[2,128,4800]{2,1,0:T(8,128)(2,1)S(1)}, bf16[2,128,4800]{2,1,0:T(8,128)(2,1)}, u32[]{:S(2)}) copy-start(bf16[2,128,4800]{2,1,0:T(8,128)(2,1)} %copy-done.1) | copy-start | bytes 7372804
  109.7 1.7 %copy-start.4 = (bf16[2,128,4800]{2,1,0:T(8,128)(2,1)S(1)}, bf16[2,128,4800]{2,1,0:T(8,128)(2,1)}, u32[]{:S(2)}) copy-start(bf16[2,128,4800]{2,1,0:T(8,128)(2,1)} %copy-done.3) | copy-start | bytes 7372804

commit v2 on v0

v2 whole, which is shorter than its diff:
```python
import functools

import jax
import jax.numpy as jnp
from jax import lax
from jax.experimental import pallas as pl
from jax.experimental.pallas import tpu as pltpu
from jax.sharding import PartitionSpec as P

MESH = pl.DeviceIdType.MESH
PIECE = 16
DEPTH = 768
F32 = jnp.float32
BF16 = jnp.bfloat16


def halves(value):
    high = value.astype(BF16)
    return high, (value - high.astype(F32)).astype(BF16)


def rows_by(left, right):
    return lax.dot_general(left, right, (((1,), (1,)), ((), ())), preferred_element_type=F32)


def plain(left, right):
    return lax.dot_general(left, right, (((1,), (0,)), ((), ())), preferred_element_type=F32)


def across(left, right):
    return lax.dot_general(left, right, (((0,), (0,)), ((), ())), preferred_element_type=F32)


def spans(count):
    return [(start, min(DEPTH, count - start)) for start in range(0, count, DEPTH)]


def exact(left, right):
    return jnp.dot(left, right, precision=lax.Precision.HIGHEST, preferred_element_type=F32)


def gather_kernel(
    peers, line, own_ref, x_ref, factors_hbm, x1, vh1, vl1, sh_ref, sl_ref,
    vt, vh0, vl0, xh, xl, part0, part1, part2, got0, got1, got2, scaled, final, gram, factors_ref,
    own_sem, factors_sem, x_sem, left_sem, right_sem, recv_sem, put_sem, got_sem,
):
    row, col = lax.axis_index("row"), lax.axis_index("col")
    columns, count = own_ref.shape[1:]
    per = columns // PIECE
    early = per // 2
    full, rest = count // DEPTH, count % DEPTH
    highs, lows = (vh0, vh1), (vl0, vl1)
    parts, gots = (part0, part1, part2), (got0, got1, got2)

    own_copy = pltpu.make_async_copy(own_ref, vt.at[col], own_sem)
    factors_copy = pltpu.make_async_copy(factors_hbm, factors_ref, factors_sem)

    def fetch(number):
        start, size = spans(count)[number]
        place = pl.ds(start, size)
        return pltpu.make_async_copy(x_ref.at[place], x1.at[place], x_sem.at[number])

    barrier = pltpu.get_barrier_semaphore()
    for offset in range(1, peers):
        pl.semaphore_signal(barrier, inc=1, device_id=(lax.rem(row + offset, peers), col), device_id_type=MESH)

    @pl.when(col > 0)
    def _():
        pl.semaphore_signal(barrier, inc=1, device_id=(row, col - 1), device_id_type=MESH)

    @pl.when(col < line - 1)
    def _():
        pl.semaphore_signal(barrier, inc=1, device_id=(row, col + 1), device_id_type=MESH)

    own_copy.start()
    for number in range(len(spans(count))):
        fetch(number).start()
    factors_copy.start()
    pl.semaphore_wait(barrier, peers - 1 + jnp.where(col > 0, 1, 0) + jnp.where(col < line - 1, 1, 0))

    def move(source, origin, panel, half, sems, away, target):
        place = pl.ds(pl.multiple_of(half * PIECE, PIECE), PIECE)
        return pltpu.make_async_remote_copy(
            src_ref=source.at[panel, place],
            dst_ref=vt.at[origin, panel, place],
            send_sem=sems.at[away, panel, half],
            recv_sem=recv_sem.at[origin, panel, half],
            device_id=(row, target),
            device_id_type=MESH,
        )

    def own_left(panel, half):
        return move(own_ref, col, panel, half, left_sem, 0, col - 1)

    def own_right(panel, half):
        return move(own_ref, col, panel, half, right_sem, 0, col + 1)

    firsts = [(0, half) for half in range(per)] + [(1, half) for half in range(early)]
    lates = [(1, half) for half in range(early, per)]

    for panel, half in firsts:
        @pl.when(col > 0)
        def _():
            own_left(panel, half).start()

        @pl.when(col < line - 1)
        def _():
            own_right(panel, half).start()

    for panel, half in lates:
        @pl.when(col == line - 1)
        def _():
            own_left(panel, half).start()

        @pl.when(col == 0)
        def _():
            own_right(panel, half).start()

    for number, (start, size) in enumerate(spans(count)):
        fetch(number).wait()

        @pl.loop(0, size // 64)
        def _(block):
            place = pl.ds(pl.multiple_of(start + block * 64, 64), 64)
            high, low = halves(x1[place])
            xh[place] = high
            xl[place] = low

    own_copy.wait()
    factors_copy.wait()

    def spread(kind, index):
        @pl.loop(1, peers)
        def _(offset):
            pltpu.make_async_remote_copy(
                src_ref=parts[kind].at[index],
                dst_ref=gots[kind].at[index, offset - 1],
                send_sem=put_sem.at[kind, index],
                recv_sem=got_sem.at[kind, index],
                device_id=(lax.rem(row + offset, peers), col),
                device_id_type=MESH,
            ).start()

    def process(origin, panel, half, pieces, project=True, overlap=False):
        index = origin * per + half
        size = pieces * PIECE
        place = pl.ds(pl.multiple_of(index * PIECE, PIECE), size)
        source = pl.ds(pl.multiple_of(half * PIECE, PIECE), size)

        def add(kind, value):
            for piece in range(pieces):
                parts[kind][index + piece] += value[piece * PIECE : (piece + 1) * PIECE]

        for piece in range(pieces):
            if project:
                parts[panel][index + piece] = jnp.zeros(parts[panel].shape[1:], F32)
            if overlap:
                parts[2][index + piece] = jnp.zeros(parts[2].shape[1:], F32)

        def block(lanes):
            if project:
                high, low = halves(vt[origin, panel, source, lanes])
                highs[panel][place, lanes] = high
                lows[panel][place, lanes] = low
            else:
                high, low = highs[panel][place, lanes], lows[panel][place, lanes]
            both = jnp.concatenate([high, low], axis=0)
            if project:
                first = plain(both, xh[lanes])
                add(panel, first[:size] + first[size:] + plain(high, xl[lanes]))
            if overlap:
                third = rows_by(both, vh0[:, lanes])
                add(2, third[:size] + third[size:] + rows_by(high, vl0[:, lanes]))

        @pl.loop(0, full)
        def _(number):
            block(pl.ds(pl.multiple_of(number * DEPTH, DEPTH), DEPTH))

        if rest:
            block(pl.ds(full * DEPTH, rest))

        for piece in range(pieces):
            if project:
                spread(panel, index + piece)
            if overlap:
                spread(2, index + piece)

    def sides(away, act):
        @pl.when(col + away < line)
        def _():
            act(col + away)

        @pl.when(col - away >= 0)
        def _():
            act(col - away)

    def receive(panel, away, half):
        right, left = col + away, col - away

        @pl.when(right < line)
        def _():
            move(own_ref, right, panel, half, left_sem, away, col).wait_recv()

            @pl.when(col > 0)
            def _():
                move(vt.at[right], right, panel, half, left_sem, away, col - 1).start()

        @pl.when(left >= 0)
        def _():
            move(own_ref, left, panel, half, right_sem, away, col).wait_recv()

            @pl.when(col < line - 1)
            def _():
                move(vt.at[left], left, panel, half, right_sem, away, col + 1).start()

    def receive_all(panel, away):
        for half in range(per):
            receive(panel, away, half)

    def collect(kind, keep):
        part, got = parts[kind], gots[kind]

        @pl.loop(0, line * per)
        def _(index):
            pltpu.make_async_copy(got.at[index], got.at[index], got_sem.at[kind, index]).wait()
            total = part[index]
            for offset in range(peers - 1):
                total = total + got[index, offset]
            keep[pl.ds(pl.multiple_of(index * PIECE, PIECE), PIECE)] = total

    process(col, 0, 0, per)

    @pl.loop(1, line)
    def _(away):
        receive_all(0, away)

        for panel, half in lates:
            @pl.when(jnp.logical_and(col + away == line - 1, col > 0))
            def _():
                own_left(panel, half).start()

            @pl.when(jnp.logical_and(col - away == 0, col < line - 1))
            def _():
                own_right(panel, half).start()

        sides(away, lambda origin: process(origin, 0, 0, per))

        @pl.when(away == 1)
        def _():
            process(col, 1, 0, per)

    def apply_first():
        collect(0, scaled)
        value = exact(factors_ref[0], scaled[...])
        scaled[...] = value
        high, low = halves(value)
        sh_ref[...] = high
        sl_ref[...] = low

        def block(lanes):
            upper, lower = vh0[:, lanes], vl0[:, lanes]
            both = jnp.concatenate([upper, lower], axis=0)
            twice = jnp.concatenate([sh_ref[...], sh_ref[...]], axis=0)
            x1[lanes] = x1[lanes] - (across(both, twice) + across(upper, sl_ref[...]))

        @pl.loop(0, full)
        def _(number):
            block(pl.ds(pl.multiple_of(number * DEPTH, DEPTH), DEPTH))

        if rest:
            block(pl.ds(full * DEPTH, rest))

        process(col, 1, 0, per, project=False, overlap=True)

    for away in range(1, line - 1):
        receive_all(1, away)
        if away == 1:
            sides(away, lambda origin: process(origin, 1, 0, per))
            apply_first()
            sides(away, lambda origin: process(origin, 1, 0, per, project=False, overlap=True))
        else:
            sides(away, lambda origin: process(origin, 1, 0, per, overlap=True))
    if line == 2:
        apply_first()
    for half in range(per):
        receive(1, line - 1, half)
        sides(line - 1, lambda origin: process(origin, 1, half, 1, overlap=True))

    collect(2, gram)
    collect(1, final)
    projection = final[...] - exact(gram[...], scaled[...])
    high, low = halves(exact(factors_ref[1], projection))
    sh_ref[...] = high
    sl_ref[...] = low

    for panel in range(2):
        for half in range(per):
            @pl.when(col > 0)
            def _():
                own_left(panel, half).wait_send()

            @pl.when(col < line - 1)
            def _():
                own_right(panel, half).wait_send()

        @pl.loop(1, line)
        def _(away):
            @pl.loop(0, per)
            def _(half):
                @pl.when(jnp.logical_and(col + away < line, col > 0))
                def _():
                    move(own_ref, col + away, panel, half, left_sem, away, col - 1).wait_send()

                @pl.when(jnp.logical_and(col - away >= 0, col < line - 1))
                def _():
                    move(own_ref, col - away, panel, half, right_sem, away, col + 1).wait_send()

    for kind in range(3):
        got = gots[kind]

        @pl.loop(0, line * per)
        def _(index):
            pltpu.make_async_copy(got.at[index], got.at[index], put_sem.at[kind, index]).wait()


def update_kernel(x_ref, vh_ref, vl_ref, sh_ref, sl_ref, out_ref, stage, sems):
    count = x_ref.shape[0]
    twice = jnp.concatenate([sh_ref[...], sh_ref[...]], axis=0)

    def put(number):
        start, size = spans(count)[number]
        return pltpu.make_async_copy(stage.at[number % 2, pl.ds(0, size)], out_ref.at[pl.ds(start, size)], sems.at[number % 2])

    numbers = range(len(spans(count)))
    for number in numbers:
        start, size = spans(count)[number]
        place = pl.ds(start, size)
        if number >= 2:
            put(number - 2).wait()
        upper = vh_ref[:, place]
        both = jnp.concatenate([upper, vl_ref[:, place]], axis=0)
        stage[number % 2, :size] = x_ref[place] - (across(both, twice) + across(upper, sl_ref[...]))
        put(number).start()
    for number in numbers[-2:]:
        put(number).wait()


def per_device(peers, line, eigvecs, panels, factors):
    count, width = eigvecs.shape
    columns = panels.shape[2]
    total = columns * line
    per = columns // PIECE
    own = jnp.swapaxes(panels, 1, 2)
    outside = pl.BlockSpec(memory_space=pltpu.HBM)
    inside = pl.BlockSpec(memory_space=pltpu.VMEM)
    pieces = line * per
    held = pl.pallas_call(
        functools.partial(gather_kernel, peers, line),
        out_shape=(
            jax.ShapeDtypeStruct((count, width), F32),
            jax.ShapeDtypeStruct((total, count), BF16),
            jax.ShapeDtypeStruct((total, count), BF16),
            jax.ShapeDtypeStruct((total, width), BF16),
            jax.ShapeDtypeStruct((total, width), BF16),
        ),
        in_specs=[outside] * 3,
        out_specs=(inside,) * 5,
        scratch_shapes=[
            pltpu.VMEM((line, 2, columns, count), F32),
            pltpu.VMEM((total, count), BF16),
            pltpu.VMEM((total, count), BF16),
            pltpu.VMEM((count, width), BF16),
            pltpu.VMEM((count, width), BF16),
            pltpu.VMEM((pieces, PIECE, width), F32),
            pltpu.VMEM((pieces, PIECE, width), F32),
            pltpu.VMEM((pieces, PIECE, total), F32),
            pltpu.VMEM((pieces, peers - 1, PIECE, width), F32),
            pltpu.VMEM((pieces, peers - 1, PIECE, width), F32),
            pltpu.VMEM((pieces, peers - 1, PIECE, total), F32),
            pltpu.VMEM((total, width), F32),
            pltpu.VMEM((total, width), F32),
            pltpu.VMEM((total, total), F32),
            pltpu.VMEM(factors.shape, F32),
            pltpu.SemaphoreType.DMA,
            pltpu.SemaphoreType.DMA,
            pltpu.SemaphoreType.DMA((len(spans(count)),)),
            pltpu.SemaphoreType.DMA((line, 2, per)),
            pltpu.SemaphoreType.DMA((line, 2, per)),
            pltpu.SemaphoreType.DMA((line, 2, per)),
            pltpu.SemaphoreType.DMA((3, pieces)),
            pltpu.SemaphoreType.DMA((3, pieces)),
        ],
        compiler_params=pltpu.CompilerParams(
            collective_id=0, has_side_effects=True, vmem_limit_bytes=30 * 1024 * 1024
        ),
        name="gather_project",
    )(*(pltpu.with_memory_space_constraint(array, pltpu.HBM) for array in (own, eigvecs, factors)))
    return pl.pallas_call(
        update_kernel,
        out_shape=jax.ShapeDtypeStruct((count, width), F32),
        in_specs=[inside] * 5,
        out_specs=outside,
        scratch_shapes=[pltpu.VMEM((2, DEPTH, width), F32), pltpu.SemaphoreType.DMA((2,))],
        compiler_params=pltpu.CompilerParams(vmem_limit_bytes=24 * 1024 * 1024),
        name="update",
    )(*held)


def solution(mesh):
    return jax.shard_map(
        functools.partial(per_device, mesh.shape["row"], mesh.shape["col"]),
        mesh=mesh,
        in_specs=(P("row", "col"), P(None, "row", "col"), P()),
        out_specs=P("row", "col"),
        check_vma=False,
    )
```

time: 284 us -> 107 us (0.38)
  waiting for transfers between devices: 197 us -> 0 us
  Pallas kernels: 0 us -> 107 us
  matrix products: 71.4 us -> 0 us
  between operations: 13.2 us -> 0.17 us
    pallas_call x0 -> x2, Pallas kernels: none -> 107 us  [the longest x1 99 us: per_device(): pl.pallas_call(functools.partial(gather_kernel, peers, line), out_shape=(...]
    psum x2 -> x0, waiting for transfers between devices: 105 us -> none  [per_device(): projection = lax.psum(inner(vectors, rotated), 'row')]
    all_gather x2 -> x0, waiting for transfers between devices: 91.3 us -> none  [per_device(): vectors = lax.all_gather(panels[index], 'col', axis=1, tiled=True)]
    dot_general x6 -> x0, matrix products: 71.4 us -> none  [the longest x2 35.8 us: inner(): lax.dot_general(left, right, (((0,), (0,)), ((), ())), precision=lax.Prec...]
  transfers between devices with their start and end apart: 4 -> 0, of which waited for: 4 -> 0; matrix products, arithmetic and copies ran while one was open for 6% -> 0% of each run, Pallas kernels for 0% -> 0%
where the time goes in v2:
time: 107 us
  Pallas kernels  107 us (100%)
    pallas_call x1, Pallas kernels, per_device(): pl.pallas_call(functools.partial(gather_kernel, peers, line), out_shape=(...  99 us
    pallas_call x1, Pallas kernels, per_device(): pl.pallas_call(update_kernel, out_shape=jax.ShapeDtypeStruct((count, widt...  7.65 us

profile of v2, /device:TPU:0, one launch (start us, length us, event | category | flops | bytes accessed | tf_op | source)
XLA Modules:
  0.0 106.8 jit_solution(5126530970846136327)
XLA Ops:
  0.0 99.0 %gather_project.1 = (f32[4800,640]{1,0:T(8,128)S(1)}, bf16[128,4800]{1,0:T(8,128)(2,1)S(1)}, bf16[128,4800]{1,0:T(8,128)(2,1)S(1)}, bf16[128,640]{1,0:T(8,128)(2,1)S(1)}, bf16[128,640]{1,0:T(8,128)(2,1)S(1)}) custom-call(f32[2,32,4800]{2,1,0:T(8,128)} %bitcast.1, f32[4800,640]{1,0:T(8,128)} %x_ref.1, f32[2,128,128]{2,1,0:T(8,128)} %factors_hbm.1), custom_call_target="tpu_custom_call" | custom-call | tf_op jit(solution)/shard_map/gather_project/pallas_call | solution.py:357
  99.0 7.6 %update.1 = f32[4800,640]{1,0:T(8,128)} custom-call(f32[4800,640]{1,0:T(8,128)S(1)} %get-tuple-element.10.x_ref, bf16[128,4800]{1,0:T(8,128)(2,1)S(1)} %get-tuple-element.11.vh_ref, bf16[128,4800]{1,0:T(8,128)(2,1)S(1)} %get-tuple-element.12.vl_ref, bf16[128,640]{1,0:T(8,128)(2,1)S(1)} %get-tuple-element.13.sh_ref, bf16[128,640]{1,0:T(8,128)(2,1)S(1)} %get-tuple-element.14.sl_ref), custom_call_target="tpu_custom_call" | custom-call | tf_op jit(solution)/shard_map/update/pallas_call | solution.py:398

commit v3 on v2

--- a/solution.py
+++ b/solution.py
@@ -19,10 +19,6 @@
     return high, (value - high.astype(F32)).astype(BF16)
 
 
-def rows_by(left, right):
-    return lax.dot_general(left, right, (((1,), (1,)), ((), ())), preferred_element_type=F32)
-
-
 def plain(left, right):
     return lax.dot_general(left, right, (((1,), (0,)), ((), ())), preferred_element_type=F32)
 
@@ -41,7 +37,7 @@
 
 def gather_kernel(
     peers, line, own_ref, x_ref, factors_hbm, x1, vh1, vl1, sh_ref, sl_ref,
-    vt, vh0, vl0, xh, xl, part0, part1, part2, got0, got1, got2, scaled, final, gram, factors_ref,
+    vt, vh0, vl0, xh, xl, part0, part1, got0, got1, scaled, factors_ref,
     own_sem, factors_sem, x_sem, left_sem, right_sem, recv_sem, put_sem, got_sem,
 ):
     row, col = lax.axis_index("row"), lax.axis_index("col")
@@ -50,7 +46,7 @@
     early = per // 2
     full, rest = count // DEPTH, count % DEPTH
     highs, lows = (vh0, vh1), (vl0, vl1)
-    parts, gots = (part0, part1, part2), (got0, got1, got2)
+    parts, gots = (part0, part1), (got0, got1)
 
     own_copy = pltpu.make_async_copy(own_ref, vt.at[col], own_sem)
     factors_copy = pltpu.make_async_copy(factors_hbm, factors_ref, factors_sem)
@@ -141,36 +137,24 @@
                 device_id_type=MESH,
             ).start()
 
-    def process(origin, panel, half, pieces, project=True, overlap=False):
+    def process(panel, origin, shards, half, pieces):
         index = origin * per + half
-        size = pieces * PIECE
+        size = shards * pieces * PIECE
         place = pl.ds(pl.multiple_of(index * PIECE, PIECE), size)
-        source = pl.ds(pl.multiple_of(half * PIECE, PIECE), size)
-
-        def add(kind, value):
-            for piece in range(pieces):
-                parts[kind][index + piece] += value[piece * PIECE : (piece + 1) * PIECE]
-
-        for piece in range(pieces):
-            if project:
-                parts[panel][index + piece] = jnp.zeros(parts[panel].shape[1:], F32)
-            if overlap:
-                parts[2][index + piece] = jnp.zeros(parts[2].shape[1:], F32)
+        source = pl.ds(pl.multiple_of(half * PIECE, PIECE), pieces * PIECE)
+        part = parts[panel]
+        number_of = shards * pieces
+        part[pl.ds(index, number_of)] = jnp.zeros((number_of,) + part.shape[1:], F32)
 
         def block(lanes):
-            if project:
-                high, low = halves(vt[origin, panel, source, lanes])
-                highs[panel][place, lanes] = high
-                lows[panel][place, lanes] = low
-            else:
-                high, low = highs[panel][place, lanes], lows[panel][place, lanes]
+            value = vt[pl.ds(origin, shards), panel, source, lanes]
+            high, low = halves(value.reshape(size, value.shape[2]))
+            highs[panel][place, lanes] = high
+            lows[panel][place, lanes] = low
             both = jnp.concatenate([high, low], axis=0)
-            if project:
-                first = plain(both, xh[lanes])
-                add(panel, first[:size] + first[size:] + plain(high, xl[lanes]))
-            if overlap:
-                third = rows_by(both, vh0[:, lanes])
-                add(2, third[:size] + third[size:] + rows_by(high, vl0[:, lanes]))
+            first = plain(both, xh[lanes])
+            total = first[:size] + first[size:] + plain(high, xl[lanes])
+            part[pl.ds(index, number_of)] += total.reshape(number_of, PIECE, total.shape[1])
 
         @pl.loop(0, full)
         def _(number):
@@ -179,20 +163,8 @@
         if rest:
             block(pl.ds(full * DEPTH, rest))
 
-        for piece in range(pieces):
-            if project:
-                spread(panel, index + piece)
-            if overlap:
-                spread(2, index + piece)
-
-    def sides(away, act):
-        @pl.when(col + away < line)
-        def _():
-            act(col + away)
-
-        @pl.when(col - away >= 0)
-        def _():
-            act(col - away)
+        for piece in range(number_of):
+            spread(panel, index + piece)
 
     def receive(panel, away, half):
         right, left = col + away, col - away
@@ -228,8 +200,6 @@
                 total = total + got[index, offset]
             keep[pl.ds(pl.multiple_of(index * PIECE, PIECE), PIECE)] = total
 
-    process(col, 0, 0, per)
-
     @pl.loop(1, line)
     def _(away):
         receive_all(0, away)
@@ -243,11 +213,7 @@
             def _():
                 own_right(panel, half).start()
 
-        sides(away, lambda origin: process(origin, 0, 0, per))
-
-        @pl.when(away == 1)
-        def _():
-            process(col, 1, 0, per)
+    process(0, 0, line, 0, per)
 
     def apply_first():
         collect(0, scaled)
@@ -261,7 +227,11 @@
             upper, lower = vh0[:, lanes], vl0[:, lanes]
             both = jnp.concatenate([upper, lower], axis=0)
             twice = jnp.concatenate([sh_ref[...], sh_ref[...]], axis=0)
-            x1[lanes] = x1[lanes] - (across(both, twice) + across(upper, sl_ref[...]))
+            value = x1[lanes] - (across(both, twice) + across(upper, sl_ref[...]))
+            x1[lanes] = value
+            high, low = halves(value)
+            xh[lanes] = high
+            xl[lanes] = low
 
         @pl.loop(0, full)
         def _(number):
@@ -270,25 +240,19 @@
         if rest:
             block(pl.ds(full * DEPTH, rest))
 
-        process(col, 1, 0, per, project=False, overlap=True)
-
-    for away in range(1, line - 1):
+    if line > 2:
+        receive_all(1, 1)
+    apply_first()
+    for away in range(2, line - 1):
         receive_all(1, away)
-        if away == 1:
-            sides(away, lambda origin: process(origin, 1, 0, per))
-            apply_first()
-            sides(away, lambda origin: process(origin, 1, 0, per, project=False, overlap=True))
-        else:
-            sides(away, lambda origin: process(origin, 1, 0, per, overlap=True))
-    if line == 2:
-        apply_first()
+    top = col == line - 1
+    process(1, jnp.where(top, 1, 0), line - 1, 0, per)
     for half in range(per):
         receive(1, line - 1, half)
-        sides(line - 1, lambda origin: process(origin, 1, half, 1, overlap=True))
-
-    collect(2, gram)
-    collect(1, final)
-    projection = final[...] - exact(gram[...], scaled[...])
+        process(1, jnp.where(top, 0, line - 1), 1, half, 1)
+
+    collect(1, scaled)
+    projection = scaled[...]
     high, low = halves(exact(factors_ref[1], projection))
     sh_ref[...] = high
     sl_ref[...] = low
@@ -315,7 +279,7 @@
                 def _():
                     move(own_ref, col - away, panel, half, right_sem, away, col + 1).wait_send()
 
-    for kind in range(3):
+    for kind in range(2):
         got = gots[kind]
 
         @pl.loop(0, line * per)
@@ -373,13 +337,9 @@
             pltpu.VMEM((count, width), BF16),
             pltpu.VMEM((pieces, PIECE, width), F32),
             pltpu.VMEM((pieces, PIECE, width), F32),
-            pltpu.VMEM((pieces, PIECE, total), F32),
             pltpu.VMEM((pieces, peers - 1, PIECE, width), F32),
             pltpu.VMEM((pieces, peers - 1, PIECE, width), F32),
-            pltpu.VMEM((pieces, peers - 1, PIECE, total), F32),
             pltpu.VMEM((total, width), F32),
-            pltpu.VMEM((total, width), F32),
-            pltpu.VMEM((total, total), F32),
             pltpu.VMEM(factors.shape, F32),
             pltpu.SemaphoreType.DMA,
             pltpu.SemaphoreType.DMA,
@@ -387,8 +347,8 @@
             pltpu.SemaphoreType.DMA((line, 2, per)),
             pltpu.SemaphoreType.DMA((line, 2, per)),
             pltpu.SemaphoreType.DMA((line, 2, per)),
-            pltpu.SemaphoreType.DMA((3, pieces)),
-            pltpu.SemaphoreType.DMA((3, pieces)),
+            pltpu.SemaphoreType.DMA((2, pieces)),
+            pltpu.SemaphoreType.DMA((2, pieces)),
         ],
         compiler_params=pltpu.CompilerParams(
             collective_id=0, has_side_effects=True, vmem_limit_bytes=30 * 1024 * 1024

time: 107 us -> 135 us (1.26)
  Pallas kernels: 107 us -> 135 us
    pallas_call x1, Pallas kernels: 99 us -> 128 us  [per_device(): pl.pallas_call(functools.partial(gather_kernel, peers, line), out_shape=(...]
where the time goes in v3:
time: 135 us
  Pallas kernels  135 us (100%)
    pallas_call x1, Pallas kernels, per_device(): pl.pallas_call(functools.partial(gather_kernel, peers, line), out_shape=(...  128 us
    pallas_call x1, Pallas kernels, per_device(): pl.pallas_call(update_kernel, out_shape=jax.ShapeDtypeStruct((count, widt...  7.65 us

profile of v3, /device:TPU:0, one launch (start us, length us, event | category | flops | bytes accessed | tf_op | source)
XLA Modules:
  0.0 135.3 jit_solution(523440007785937217)
XLA Ops:
  0.0 127.6 %gather_project.1 = (f32[4800,640]{1,0:T(8,128)S(1)}, bf16[128,4800]{1,0:T(8,128)(2,1)S(1)}, bf16[128,4800]{1,0:T(8,128)(2,1)S(1)}, bf16[128,640]{1,0:T(8,128)(2,1)S(1)}, bf16[128,640]{1,0:T(8,128)(2,1)S(1)}) custom-call(f32[2,32,4800]{2,1,0:T(8,128)} %bitcast.1, f32[4800,640]{1,0:T(8,128)} %x_ref.1, f32[2,128,128]{2,1,0:T(8,128)} %factors_hbm.1), custom_call_target="tpu_custom_call" | custom-call | tf_op jit(solution)/shard_map/gather_project/pallas_call | solution.py:321
  127.6 7.6 %update.1 = f32[4800,640]{1,0:T(8,128)} custom-call(f32[4800,640]{1,0:T(8,128)S(1)} %get-tuple-element.10.x_ref, bf16[128,4800]{1,0:T(8,128)(2,1)S(1)} %get-tuple-element.11.vh_ref, bf16[128,4800]{1,0:T(8,128)(2,1)S(1)} %get-tuple-element.12.vl_ref, bf16[128,640]{1,0:T(8,128)(2,1)S(1)} %get-tuple-element.13.sh_ref, bf16[128,640]{1,0:T(8,128)(2,1)S(1)} %get-tuple-element.14.sl_ref), custom_call_target="tpu_custom_call" | custom-call | tf_op jit(solution)/shard_map/update/pallas_call | solution.py:358

commit v4 on v2

--- a/solution.py
+++ b/solution.py
@@ -41,7 +41,7 @@
 
 def gather_kernel(
     peers, line, own_ref, x_ref, factors_hbm, x1, vh1, vl1, sh_ref, sl_ref,
-    vt, vh0, vl0, xh, xl, part0, part1, part2, got0, got1, got2, scaled, final, gram, factors_ref,
+    vt, vh0, vl0, xh, xl, part0, part1, part2, got0, got1, got2, scaled, final, factors_ref,
     own_sem, factors_sem, x_sem, left_sem, right_sem, recv_sem, put_sem, got_sem,
 ):
     row, col = lax.axis_index("row"), lax.axis_index("col")
@@ -217,16 +217,13 @@
         for half in range(per):
             receive(panel, away, half)
 
-    def collect(kind, keep):
-        part, got = parts[kind], gots[kind]
-
-        @pl.loop(0, line * per)
-        def _(index):
-            pltpu.make_async_copy(got.at[index], got.at[index], got_sem.at[kind, index]).wait()
-            total = part[index]
-            for offset in range(peers - 1):
-                total = total + got[index, offset]
-            keep[pl.ds(pl.multiple_of(index * PIECE, PIECE), PIECE)] = total
+    def gather_sum(kind, index):
+        got = gots[kind]
+        pltpu.make_async_copy(got.at[index], got.at[index], got_sem.at[kind, index]).wait()
+        total = parts[kind][index]
+        for offset in range(peers - 1):
+            total = total + got[index, offset]
+        return total
 
     process(col, 0, 0, per)
 
@@ -250,7 +247,10 @@
             process(col, 1, 0, per)
 
     def apply_first():
-        collect(0, scaled)
+        @pl.loop(0, line * per)
+        def _(index):
+            scaled[pl.ds(pl.multiple_of(index * PIECE, PIECE), PIECE)] = gather_sum(0, index)
+
         value = exact(factors_ref[0], scaled[...])
         scaled[...] = value
         high, low = halves(value)
@@ -282,14 +282,27 @@
             sides(away, lambda origin: process(origin, 1, 0, per, overlap=True))
     if line == 2:
         apply_first()
+
+    def settle(index):
+        corrected = gather_sum(1, index) - exact(gather_sum(2, index), scaled[...])
+        final[pl.ds(pl.multiple_of(index * PIECE, PIECE), PIECE)] = corrected
+
+    @pl.loop(0, line)
+    def _(origin):
+        @pl.when(jnp.logical_and(origin - col < line - 1, col - origin < line - 1))
+        def _():
+            @pl.loop(0, per)
+            def _(half):
+                settle(origin * per + half)
+
     for half in range(per):
         receive(1, line - 1, half)
         sides(line - 1, lambda origin: process(origin, 1, half, 1, overlap=True))
-
-    collect(2, gram)
-    collect(1, final)
-    projection = final[...] - exact(gram[...], scaled[...])
-    high, low = halves(exact(factors_ref[1], projection))
+        if half < per - 1:
+            sides(line - 1, lambda origin: settle(origin * per + half))
+    sides(line - 1, lambda origin: settle(origin * per + per - 1))
+
+    high, low = halves(exact(factors_ref[1], final[...]))
     sh_ref[...] = high
     sl_ref[...] = low
 
@@ -379,7 +392,6 @@
             pltpu.VMEM((pieces, peers - 1, PIECE, total), F32),
             pltpu.VMEM((total, width), F32),
             pltpu.VMEM((total, width), F32),
-            pltpu.VMEM((total, total), F32),
             pltpu.VMEM(factors.shape, F32),
             pltpu.SemaphoreType.DMA,
             pltpu.SemaphoreType.DMA,

time: 107 us -> 118 us (1.10)
  Pallas kernels: 107 us -> 118 us
    pallas_call x1, Pallas kernels: 99 us -> 110 us  [per_device(): pl.pallas_call(functools.partial(gather_kernel, peers, line), out_shape=(...]
where the time goes in v4:
time: 118 us
  Pallas kernels  118 us (100%)
    pallas_call x1, Pallas kernels, per_device(): pl.pallas_call(functools.partial(gather_kernel, peers, line), out_shape=(...  110 us
    pallas_call x1, Pallas kernels, per_device(): pl.pallas_call(update_kernel, out_shape=jax.ShapeDtypeStruct((count, widt...  7.65 us

profile of v4, /device:TPU:0, one launch (start us, length us, event | category | flops | bytes accessed | tf_op | source)
XLA Modules:
  0.0 118.3 jit_solution(10883492802124997938)
XLA Ops:
  0.0 110.5 %gather_project.1 = (f32[4800,640]{1,0:T(8,128)S(1)}, bf16[128,4800]{1,0:T(8,128)(2,1)S(1)}, bf16[128,4800]{1,0:T(8,128)(2,1)S(1)}, bf16[128,640]{1,0:T(8,128)(2,1)S(1)}, bf16[128,640]{1,0:T(8,128)(2,1)S(1)}) custom-call(f32[2,32,4800]{2,1,0:T(8,128)} %bitcast.1, f32[4800,640]{1,0:T(8,128)} %x_ref.1, f32[2,128,128]{2,1,0:T(8,128)} %factors_hbm.1), custom_call_target="tpu_custom_call" | custom-call | tf_op jit(solution)/shard_map/gather_project/pallas_call | solution.py:370
  110.5 7.6 %update.1 = f32[4800,640]{1,0:T(8,128)} custom-call(f32[4800,640]{1,0:T(8,128)S(1)} %get-tuple-element.10.x_ref, bf16[128,4800]{1,0:T(8,128)(2,1)S(1)} %get-tuple-element.11.vh_ref, bf16[128,4800]{1,0:T(8,128)(2,1)S(1)} %get-tuple-element.12.vl_ref, bf16[128,640]{1,0:T(8,128)(2,1)S(1)} %get-tuple-element.13.sh_ref, bf16[128,640]{1,0:T(8,128)(2,1)S(1)} %get-tuple-element.14.sl_ref), custom_call_target="tpu_custom_call" | custom-call | tf_op jit(solution)/shard_map/update/pallas_call | solution.py:410

commit v5 on v4

--- a/solution.py
+++ b/solution.py
@@ -41,7 +41,7 @@
 
 def gather_kernel(
     peers, line, own_ref, x_ref, factors_hbm, x1, vh1, vl1, sh_ref, sl_ref,
-    vt, vh0, vl0, xh, xl, part0, part1, part2, got0, got1, got2, scaled, final, factors_ref,
+    vt, vh0, vl0, xh, xl, part0, part1, part2, got0, got1, got2, scaled, final, gram, factors_ref,
     own_sem, factors_sem, x_sem, left_sem, right_sem, recv_sem, put_sem, got_sem,
 ):
     row, col = lax.axis_index("row"), lax.axis_index("col")
@@ -284,8 +284,9 @@
         apply_first()
 
     def settle(index):
-        corrected = gather_sum(1, index) - exact(gather_sum(2, index), scaled[...])
-        final[pl.ds(pl.multiple_of(index * PIECE, PIECE), PIECE)] = corrected
+        place = pl.ds(pl.multiple_of(index * PIECE, PIECE), PIECE)
+        final[place] = gather_sum(1, index)
+        gram[place] = gather_sum(2, index)
 
     @pl.loop(0, line)
     def _(origin):
@@ -298,11 +299,11 @@
     for half in range(per):
         receive(1, line - 1, half)
         sides(line - 1, lambda origin: process(origin, 1, half, 1, overlap=True))
-        if half < per - 1:
-            sides(line - 1, lambda origin: settle(origin * per + half))
-    sides(line - 1, lambda origin: settle(origin * per + per - 1))
-
-    high, low = halves(exact(factors_ref[1], final[...]))
+    for half in range(per):
+        sides(line - 1, lambda origin: settle(origin * per + half))
+
+    projection = final[...] - exact(gram[...], scaled[...])
+    high, low = halves(exact(factors_ref[1], projection))
     sh_ref[...] = high
     sl_ref[...] = low
 
@@ -392,6 +393,7 @@
             pltpu.VMEM((pieces, peers - 1, PIECE, total), F32),
             pltpu.VMEM((total, width), F32),
             pltpu.VMEM((total, width), F32),
+            pltpu.VMEM((total, total), F32),
             pltpu.VMEM(factors.shape, F32),
             pltpu.SemaphoreType.DMA,
             pltpu.SemaphoreType.DMA,

time: 118 us -> 112 us (0.949)
  Pallas kernels: 118 us -> 112 us
    pallas_call x1, Pallas kernels: 110 us -> 104 us  [per_device(): pl.pallas_call(functools.partial(gather_kernel, peers, line), out_shape=(...]
where the time goes in v5:
time: 112 us
  Pallas kernels  112 us (100%)
    pallas_call x1, Pallas kernels, per_device(): pl.pallas_call(functools.partial(gather_kernel, peers, line), out_shape=(...  104 us
    pallas_call x1, Pallas kernels, per_device(): pl.pallas_call(update_kernel, out_shape=jax.ShapeDtypeStruct((count, widt...  7.65 us

profile of v5, /device:TPU:0, one launch (start us, length us, event | category | flops | bytes accessed | tf_op | source)
XLA Modules:
  0.0 112.2 jit_solution(3031841431086317750)
XLA Ops:
  0.0 104.4 %gather_project.1 = (f32[4800,640]{1,0:T(8,128)S(1)}, bf16[128,4800]{1,0:T(8,128)(2,1)S(1)}, bf16[128,4800]{1,0:T(8,128)(2,1)S(1)}, bf16[128,640]{1,0:T(8,128)(2,1)S(1)}, bf16[128,640]{1,0:T(8,128)(2,1)S(1)}) custom-call(f32[2,32,4800]{2,1,0:T(8,128)} %bitcast.1, f32[4800,640]{1,0:T(8,128)} %x_ref.1, f32[2,128,128]{2,1,0:T(8,128)} %factors_hbm.1), custom_call_target="tpu_custom_call" | custom-call | tf_op jit(solution)/shard_map/gather_project/pallas_call | solution.py:371
  104.4 7.6 %update.1 = f32[4800,640]{1,0:T(8,128)} custom-call(f32[4800,640]{1,0:T(8,128)S(1)} %get-tuple-element.10.x_ref, bf16[128,4800]{1,0:T(8,128)(2,1)S(1)} %get-tuple-element.11.vh_ref, bf16[128,4800]{1,0:T(8,128)(2,1)S(1)} %get-tuple-element.12.vl_ref, bf16[128,640]{1,0:T(8,128)(2,1)S(1)} %get-tuple-element.13.sh_ref, bf16[128,640]{1,0:T(8,128)(2,1)S(1)} %get-tuple-element.14.sl_ref), custom_call_target="tpu_custom_call" | custom-call | tf_op jit(solution)/shard_map/update/pallas_call | solution.py:412
